TPU v7x, 256 devices: a whole 4x4x8 slice. The times are simulated.
256 devices in a mesh: seq: 64 (over y_hi, x, z), head: 4 (over y_lo, core).
Axes of the slice: x: 4, y: 4 (y_hi: 2, y_lo: 2; y = y_hi * 2 + y_lo), z: 8, core: 2. Of those that a mesh axis runs over, the one named last changes fastest.
Arguments:
- queries: bfloat16 [16384, 1024], P('seq', 'head'), may hold values from -40 to 40
- keys: bfloat16 [16384, 1024], P('seq', 'head'), may hold values from -12 to 12
- values: bfloat16 [16384, 1024], P('seq', 'head'), may hold values from -6 to 6
- residual: bfloat16 [16384, 1024], P('seq', 'head'), may hold values from -3 to 3
- reg_weight: bfloat16 [1024, 1024], P('head'), may hold values from -0.1875 to 0.1875
- targets: bfloat16 [256, 16, 1024], P('seq'), may hold values from -3 to 3
- block_track: int32 [128], replicated, may hold values from 0 to 255
- row_count: int32 [128], P('seq'), may hold values from 1 to 128, 12288 in all
- pool_slot: int32 [128, 128], P('seq'), may hold values from 0 to 15
Outputs:
- grad_reg: bfloat16 [1024, 1024], P('head')
- context_grad: bfloat16 [16384, 1024], P('seq', 'head')
All inputs are finite; a program needn't handle non-finite values. No bound on the sum of `row_count` on one device may be relied on, other than what follows from the above.
Results may differ from a plain program's by a relative error of at most 0.019.
Values may be sent and summed in bfloat16 or wider, within the bound.
No kernel may reach another device: no remote copies, remote signals or barrier semaphores. Data moves between devices by JAX's collectives and lax.ppermute only.
A program may use at most 128 MiB of HBM per device.

v0:
```python
import jax
import jax.numpy as jnp
from jax import lax
from jax.sharding import PartitionSpec as P

HEAD_DIM = 64
BLK = 128
POOL = 16


def make_advance(query_heads, scale):

    def advance(state, block):
        run_max, run_total, run_sum = state
        key_rows, value_rows = block
        scores = (
            jnp.einsum("qhd,khd->hqk", query_heads, key_rows, preferred_element_type=jnp.float32)
            * scale
        )
        new_max = jnp.maximum(run_max, jnp.max(scores, axis=2))
        shrink = jnp.exp(run_max - new_max)
        exp_terms = jnp.exp(scores - new_max[:, :, None])
        run_total = run_total * shrink + jnp.sum(exp_terms, axis=2)
        weighted = jnp.einsum(
            "hqk,khd->hqd",
            exp_terms.astype(jnp.bfloat16),
            value_rows,
            preferred_element_type=jnp.float32,
        )
        run_sum = run_sum * shrink[:, :, None] + weighted
        return ((new_max, run_total, run_sum), None)

    return advance


def local(queries, keys, values, residual, reg_weight, targets, block_track, row_count, pool_slot):
    tok_rows, width = queries.shape
    head_count = width // HEAD_DIM
    query_heads = queries.reshape(tok_rows, head_count, HEAD_DIM)
    advance = make_advance(query_heads, HEAD_DIM ** (-0.5))
    initial = (
        jnp.full((head_count, tok_rows), -1e30, jnp.float32),
        jnp.zeros((head_count, tok_rows), jnp.float32),
        jnp.zeros((head_count, tok_rows, HEAD_DIM), jnp.float32),
    )
    state = initial
    key_piece = lax.all_gather(keys, "seq", axis=0, tiled=True)
    value_piece = lax.all_gather(values, "seq", axis=0, tiled=True)
    key_count = key_piece.shape[0]
    key_heads = key_piece.reshape(key_count, head_count, HEAD_DIM)
    value_heads = value_piece.reshape(key_count, head_count, HEAD_DIM)
    block_count = key_count // 512
    blocks = (
        key_heads.reshape(block_count, 512, head_count, HEAD_DIM),
        value_heads.reshape(block_count, 512, head_count, HEAD_DIM),
    )
    state, unused = lax.scan(advance, state, blocks)
    run_max, run_total, run_sum = state
    context = (
        (run_sum / run_total[:, :, None])
        .transpose(1, 0, 2)
        .reshape(tok_rows, width)
        .astype(jnp.bfloat16)
    )
    stream = (residual.astype(jnp.float32) + context.astype(jnp.float32)).astype(jnp.bfloat16)
    block_here = tok_rows // BLK
    owned = 2 * block_here
    seq_count = lax.axis_size("seq")
    tracks_all = owned * seq_count
    seq_index = lax.axis_index("seq")
    stream_blocks = stream.reshape(block_here, BLK, width)
    valid = jnp.arange(BLK, dtype=jnp.int32)[None, :] < row_count[:, None]
    match = pool_slot[:, None, :] == jnp.arange(POOL, dtype=jnp.int32)[None, :, None]
    selector = jnp.where(match & valid[:, None, :], 1.0, 0.0).astype(jnp.bfloat16)
    pooled = jnp.einsum("bpr,brc->bpc", selector, stream_blocks, preferred_element_type=jnp.float32)
    slot_rows = jnp.sum(selector.astype(jnp.float32), axis=2)
    own_track = lax.dynamic_slice_in_dim(block_track, seq_index * block_here, block_here)
    track_select = jnp.where(
        own_track[:, None] == jnp.arange(tracks_all, dtype=jnp.int32)[None, :], 1.0, 0.0
    ).astype(jnp.float32)
    dense_sums = jnp.einsum("bt,bpc->tpc", track_select, pooled, precision=lax.Precision.HIGHEST)
    dense_counts = jnp.einsum("bt,bp->tp", track_select, slot_rows, precision=lax.Precision.HIGHEST)
    sums, counts = (
        lax.psum_scatter(dense_sums, "seq", scatter_dimension=0, tiled=True),
        lax.psum_scatter(dense_counts, "seq", scatter_dimension=0, tiled=True),
    )
    divisor = jnp.maximum(counts, 1.0)
    mean = (sums / divisor[:, :, None]).astype(jnp.bfloat16).reshape(owned * POOL, width)
    partial_pred = jnp.dot(mean, reg_weight, preferred_element_type=jnp.float32)
    prediction = lax.psum(partial_pred.astype(jnp.bfloat16), "head").astype(jnp.float32)
    error = (prediction - targets.reshape(owned * POOL, -1).astype(jnp.float32)).astype(
        jnp.bfloat16
    )
    reg_part = lax.dot_general(
        mean, error, (((0,), (0,)), ((), ())), preferred_element_type=jnp.float32
    )
    mean_grad = lax.dot_general(
        error, reg_weight, (((1,), (1,)), ((), ())), preferred_element_type=jnp.float32
    )
    track_grad = (mean_grad.reshape(owned, POOL, width) / divisor[:, :, None]).astype(jnp.bfloat16)
    every_grad = lax.all_gather(track_grad, "seq", axis=0, tiled=True)
    grad_select = jnp.where(
        own_track[:, None] == jnp.arange(tracks_all, dtype=jnp.int32)[None, :], 1.0, 0.0
    ).astype(jnp.bfloat16)
    pooled_grad = jnp.einsum(
        "bt,tpc->bpc", grad_select, every_grad, preferred_element_type=jnp.float32
    ).astype(jnp.bfloat16)
    row_grad = jnp.einsum("bpr,bpc->brc", selector, pooled_grad, preferred_element_type=jnp.float32)
    context_grad = row_grad.reshape(tok_rows, width).astype(jnp.bfloat16)
    grad_reg = lax.psum(reg_part, "seq").astype(jnp.bfloat16)
    return (grad_reg, context_grad)


def solution(mesh):
    return jax.shard_map(
        local,
        mesh=mesh,
        in_specs=(
            P("seq", "head"),
            P("seq", "head"),
            P("seq", "head"),
            P("seq", "head"),
            P("head", None),
            P("seq", None, None),
            P(),
            P("seq"),
            P("seq", None),
        ),
        out_specs=(P("head", None), P("seq", "head")),
        check_vma=False,
    )
```

profile of v0, /device:TPU:8, one launch (start us, length us, event | category | flops | bytes accessed | tf_op | source)
XLA Modules:
  0.0 1257.6 jit_solution(4644142932304192094)
XLA Ops:
  11.2 149.7 %all-gather.4.cloned.1.call-done = bf16[16384,256]{1,0:T(8,128)(2,1)} async-done(((bf16[256,256]{1,0:T(8,128)(2,1)}), bf16[16384,256]{1,0:T(8,128)(2,1)}) %all-gather.4.cloned.1.call-update) | async-done | bytes 8388624 | tf_op jit(solution)/shard_map/all_gather | solution.py:47
  160.9 24.5 %reshape.56 = bf16[32,512,4,64]{3,2,1,0:T(4,128)(2,1)} reshape(bf16[16384,256]{1,0:T(8,128)(2,1)} %all-gather.4.cloned.1.call-done) | data formatting | bytes 16777216 | tf_op jit(solution)/shard_map/reshape;reshape | solution.py:54
  185.4 24.2 %copy.29 = bf16[32,512,4,64]{1,3,2,0:T(8,128)(2,1)} copy(bf16[32,512,4,64]{3,2,1,0:T(4,128)(2,1)} %reshape.56) | data formatting | bytes 16777216
  209.6 99.0 %all-gather.6.cloned.1.call-done = bf16[16384,256]{1,0:T(8,128)(2,1)} async-done(((bf16[256,256]{1,0:T(8,128)(2,1)}), bf16[16384,256]{1,0:T(8,128)(2,1)}) %all-gather.6.cloned.1.call-update) | async-done | bytes 8388624 | tf_op jit(solution)/shard_map/all_gather | solution.py:48
  308.6 24.5 %reshape.57 = bf16[32,512,4,64]{3,2,1,0:T(4,128)(2,1)} reshape(bf16[16384,256]{1,0:T(8,128)(2,1)} %all-gather.6.cloned.1.call-done) | data formatting | bytes 16777216 | tf_op jit(solution)/shard_map/reshape;reshape | solution.py:55
  333.1 24.2 %copy.30 = bf16[32,512,4,64]{1,3,2,0:T(8,128)(2,1)} copy(bf16[32,512,4,64]{3,2,1,0:T(4,128)(2,1)} %reshape.57) | data formatting | bytes 16777216
  357.4 107.5 %while.15 = (s32[]{:T(128)}, f32[4,256]{1,0:T(4,128)S(1)}, f32[4,256]{1,0:T(4,128)S(1)}, f32[4,256,64]{1,2,0:T(8,128)S(1)}, bf16[32,512,4,64]{1,3,2,0:T(8,128)(2...) while((s32[]{:T(128)}, f32[4,256]{1,0:T(4,128)S(1)}, ...), condition=%wide.region_3.4_spmd.clone, body=%wide.region_0.3_spmd.clone.sunk | while | flops 138613760 | bytes 7537769 | solution.py:57
  357.4 1.5 bitcast_reduce_fusion.2
  359.2 1.5 convolution_add_fusion.2
  362.6 1.5 convolution_add_fusion.2
  366.0 1.5 convolution_add_fusion.2
  369.3 1.5 convolution_add_fusion.2
  372.7 1.5 convolution_add_fusion.2
  376.0 1.5 convolution_add_fusion.2
  379.4 1.5 convolution_add_fusion.2
  382.8 1.5 convolution_add_fusion.2
  386.1 1.5 convolution_add_fusion.2
  389.5 1.5 convolution_add_fusion.2
  392.8 1.5 convolution_add_fusion.2
  396.2 1.5 convolution_add_fusion.2
  399.6 1.5 convolution_add_fusion.2
  402.9 1.5 convolution_add_fusion.2
  406.3 1.5 convolution_add_fusion.2
  409.6 1.5 convolution_add_fusion.2
  413.0 1.5 convolution_add_fusion.2
  465.3 3.8 fusion.22
  469.0 4.4 copy.33
  475.8 356.0 %all-reduce = f32[256,16]{1,0:T(8,128)S(1)} all-reduce(f32[256,16]{1,0:T(8,128)S(1)} %fusion.37), channel_id=3, replica_groups=mesh['seq'=64,'head'=4] {'seq'}, use_global_device_ids=true, to_apply=%region_6.7.clone | all-reduce | flops 4096 | bytes 32768
  831.8 8.9 reduce-scatter.2.cloned.1.call-done
  842.6 34.6 %all-reduce.4.cloned.1.call-done = bf16[64,1024]{1,0:T(8,128)(2,1)} async-done(((bf16[64,1024]{1,0:T(8,128)(2,1)}), bf16[64,1024]{1,0:T(8,128)(2,1)}) %all-reduce.4.cloned.1.call-update) | async-done | bytes 131088 | tf_op jit(solution)/shard_map/psum | solution.py:90
  879.5 368.4 %all-reduce.5 = bf16[256,1024]{1,0:T(8,128)(2,1)} all-reduce(f32[256,1024]{1,0:T(8,128)S(1)} %fusion.59), channel_id=1, replica_groups=mesh['seq'=64,'head'=4] {'seq'}, use_global_device_ids=true, to_apply=%region_8.9 | all-reduce | flops 262144 | bytes 1572864 | tf_op jit(solution)/shard_map/psum | solution.py:110
  1247.9 2.3 fusion.17
  (216 shorter events, 90.6 us)
Async XLA Ops:
  7.2 834.5 %copy-start = (bf16[256,1024]{1,0:T(8,128)(2,1)S(1)}, bf16[256,1024]{1,0:T(8,128)(2,1)}, u32[]{:S(2)}) copy-start(bf16[256,1024]{1,0:T(8,128)(2,1)} %param.15) | copy-start | bytes 1572868
  7.2 153.7 %all-gather.4.cloned.1.call-start = ((), (), s32[]{:S(2)}) async-start(), calls=%async_computation.1 | async-start | bytes 8519680 | tf_op jit(solution)/shard_map/all_gather | solution.py:47
  7.9 300.7 %all-gather.6.cloned.1.call-start = ((), (), s32[]{:S(2)}) async-start(), calls=%async_computation.2 | async-start | bytes 8519680 | tf_op jit(solution)/shard_map/all_gather | solution.py:48
  8.7 832.1 %reduce-scatter.2.cloned.1.call-start = ((), (), s32[]{:S(2)}) async-start(), calls=%async_computation.3 | async-start | bytes 4259840 | tf_op jit(solution)/shard_map/reduce_scatter | solution.py:84
  357.4 107.7 %copy-start.2 = (bf16[256,256]{1,0:T(8,128)(2,1)S(1)}, bf16[256,256]{1,0:T(8,128)(2,1)}, u32[]{:S(2)}) copy-start(bf16[256,256]{1,0:T(8,128)(2,1)} %param.14) | copy-start | bytes 393220
  357.4 107.8 %copy-start.3 = (s32[2,128]{1,0:T(2,128)S(1)}, s32[2,128]{1,0:T(2,128)}, u32[]{:S(2)}) copy-start(s32[2,128]{1,0:T(2,128)} %param.19) | copy-start | bytes 3076
  473.4 0.7 copy-start.4
  473.4 403.8 %copy-start.1 = (bf16[4,16,1024]{2,1,0:T(8,128)(2,1)S(1)}, bf16[4,16,1024]{2,1,0:T(8,128)(2,1)}, u32[]{:S(2)}) copy-start(bf16[4,16,1024]{2,1,0:T(8,128)(2,1)} %param.16) | copy-start | bytes 393220
  473.4 403.8 %all-reduce.4.cloned.1.call-start = ((), (), s32[]{:S(2)}) async-start(), calls=%async_computation.4 | async-start | bytes 262144 | tf_op jit(solution)/shard_map/psum | solution.py:90
  842.6 405.3 %all-gather.8.cloned.1.call-start = ((), (), s32[]{:S(2)}) async-start(), calls=%async_computation.5 | async-start | bytes 2129920 | tf_op jit(solution)/shard_map/all_gather | solution.py:101
Sparse Core Ops, SparseCore 0:
  11.7 149.1 all-gather.3
  164.5 144.0 all-gather.5
  473.6 367.1 reduce-scatter.1
  844.0 33.2 all-reduce.3
  881.4 118.9 all-gather.7
where the time goes:
time: 1260 us
  blocking collectives  724 us (57%)
  waiting for transfers between devices  294 us (23%)
  local copies, waits for them, and re-layouts  105 us (8%)
  matrix products  102 us (8%)
  other arithmetic  15.8 us (1%)
  between operations  14.6 us (1%)
    psum x1, blocking collectives, local(): grad_reg = lax.psum(reg_part, 'seq').astype(jnp.bfloat16)  368 us
    unnamed x1, blocking collectives  356 us
    all_gather x1, waiting for transfers between devices, local(): key_piece = lax.all_gather(keys, 'seq', axis=0, tiled=True)  150 us
    all_gather x1, waiting for transfers between devices, local(): value_piece = lax.all_gather(values, 'seq', axis=0, tiled=True)  99 us
    unnamed x14, local copies, waits for them, and re-layouts  50.6 us
    dot_general x32, matrix products, advance(): jnp.einsum('hqk,khd->hqd', exp_terms.astype(jnp.bfloat16), value_rows, pr...  46.9 us
    dot_general x32, matrix products, advance(): jnp.einsum('qhd,khd->hqk', query_heads, key_rows, preferred_element_type=...  46.6 us
    psum x1, waiting for transfers between devices, local(): lax.psum(partial_pred.astype(jnp.bfloat16), 'head').astype(jnp.float32)  34.6 us
  transfers between devices with their start and end apart: 5, of which 4 were waited for; matrix products, arithmetic and copies ran while one was open for 4% of the time, Pallas kernels for 0%

commit v1 on v0

--- a/solution.py
+++ b/solution.py
@@ -107,7 +107,7 @@
     ).astype(jnp.bfloat16)
     row_grad = jnp.einsum("bpr,bpc->brc", selector, pooled_grad, preferred_element_type=jnp.float32)
     context_grad = row_grad.reshape(tok_rows, width).astype(jnp.bfloat16)
-    grad_reg = lax.psum(reg_part, "seq").astype(jnp.bfloat16)
+    grad_reg = jnp.sum(lax.all_gather(reg_part, "seq"), axis=0).astype(jnp.bfloat16)
     return (grad_reg, context_grad)
 
 

time: 1260 us -> 1610 us (1.28)
  waiting for transfers between devices: 294 us -> 982 us
  blocking collectives: 724 us -> 356 us
  other arithmetic: 15.8 us -> 37.4 us
    all_gather x0 -> x1, waiting for transfers between devices: none -> 569 us  [local(): lax.all_gather(reg_part, 'seq')]
    psum x1 -> x0, blocking collectives: 368 us -> none  [local(): grad_reg = lax.psum(reg_part, 'seq').astype(jnp.bfloat16)]
    all_gather x1, waiting for transfers between devices: 0.01 us -> 120 us  [local(): every_grad = lax.all_gather(track_grad, 'seq', axis=0, tiled=True)]
    all_gather x1, waiting for transfers between devices: 99 us -> 150 us  [local(): value_piece = lax.all_gather(values, 'seq', axis=0, tiled=True)]
    all_gather x1, waiting for transfers between devices: 150 us -> 99 us  [local(): key_piece = lax.all_gather(keys, 'seq', axis=0, tiled=True)]
    reduce_sum x0 -> x1, other arithmetic: none -> 21.6 us  [local(): jnp.sum(lax.all_gather(reg_part, 'seq'), axis=0).astype(jnp.bfloat16)]
  transfers between devices with their start and end apart: 5 -> 6, of which waited for: 4 -> 6; matrix products, arithmetic and copies ran while one was open for 4% -> 4% of each run, Pallas kernels for 0% -> 0%
where the time goes in v1:
time: 1610 us; the launch traced here: 1600 us
  waiting for transfers between devices  982 us (61%)
  blocking collectives  356 us (22%)
  local copies, waits for them, and re-layouts  105 us (7%)
  matrix products  104 us (6%)
  other arithmetic  37.4 us (2%)
    all_gather x1, waiting for transfers between devices, local(): lax.all_gather(reg_part, 'seq')  569 us
    unnamed x1, blocking collectives  356 us
    all_gather x1, waiting for transfers between devices, local(): value_piece = lax.all_gather(values, 'seq', axis=0, tiled=True)  150 us
    all_gather x1, waiting for transfers between devices, local(): every_grad = lax.all_gather(track_grad, 'seq', axis=0, tiled=True)  120 us
    all_gather x1, waiting for transfers between devices, local(): key_piece = lax.all_gather(keys, 'seq', axis=0, tiled=True)  99 us
    unnamed x14, local copies, waits for them, and re-layouts  50.6 us
    dot_general x32, matrix products, advance(): jnp.einsum('hqk,khd->hqd', exp_terms.astype(jnp.bfloat16), value_rows, pr...  47.1 us
    dot_general x32, matrix products, advance(): jnp.einsum('qhd,khd->hqk', query_heads, key_rows, preferred_element_type=...  46.6 us
  transfers between devices with their start and end apart: 6, of which 6 were waited for; matrix products, arithmetic and copies ran while one was open for 4% of the time, Pallas kernels for 0%

profile of v1, /device:TPU:8, one launch (start us, length us, event | category | flops | bytes accessed | tf_op | source)
XLA Modules:
  0.0 1600.6 jit_solution(6876752582559564711)
XLA Ops:
  11.2 149.7 %all-gather.8.cloned.1.call-done = bf16[16384,256]{1,0:T(8,128)(2,1)} async-done(((bf16[256,256]{1,0:T(8,128)(2,1)}), bf16[16384,256]{1,0:T(8,128)(2,1)}) %all-gather.8.cloned.1.call-update) | async-done | bytes 8388624 | tf_op jit(solution)/shard_map/all_gather | solution.py:48
  160.9 24.5 %reshape.58 = bf16[32,512,4,64]{3,2,1,0:T(4,128)(2,1)} reshape(bf16[16384,256]{1,0:T(8,128)(2,1)} %all-gather.8.cloned.1.call-done) | data formatting | bytes 16777216 | tf_op jit(solution)/shard_map/reshape;reshape | solution.py:55
  185.4 24.2 %copy.30 = bf16[32,512,4,64]{1,3,2,0:T(8,128)(2,1)} copy(bf16[32,512,4,64]{3,2,1,0:T(4,128)(2,1)} %reshape.58) | data formatting | bytes 16777216
  209.6 99.0 %all-gather.6.cloned.1.call-done = bf16[16384,256]{1,0:T(8,128)(2,1)} async-done(((bf16[256,256]{1,0:T(8,128)(2,1)}), bf16[16384,256]{1,0:T(8,128)(2,1)}) %all-gather.6.cloned.1.call-update) | async-done | bytes 8388624 | tf_op jit(solution)/shard_map/all_gather | solution.py:47
  308.6 24.5 %reshape.57 = bf16[32,512,4,64]{3,2,1,0:T(4,128)(2,1)} reshape(bf16[16384,256]{1,0:T(8,128)(2,1)} %all-gather.6.cloned.1.call-done) | data formatting | bytes 16777216 | tf_op jit(solution)/shard_map/reshape;reshape | solution.py:54
  333.1 24.2 %copy.29 = bf16[32,512,4,64]{1,3,2,0:T(8,128)(2,1)} copy(bf16[32,512,4,64]{3,2,1,0:T(4,128)(2,1)} %reshape.57) | data formatting | bytes 16777216
  357.4 107.5 %while.15 = (s32[]{:T(128)}, f32[4,256]{1,0:T(4,128)S(1)}, f32[4,256]{1,0:T(4,128)S(1)}, f32[4,256,64]{1,2,0:T(8,128)S(1)}, bf16[32,512,4,64]{1,3,2,0:T(8,128)(2...) while((s32[]{:T(128)}, f32[4,256]{1,0:T(4,128)S(1)}, ...), condition=%wide.region_3.4_spmd.clone, body=%wide.region_0.3_spmd.clone.sunk | while | flops 138613760 | bytes 7536761 | solution.py:57
  357.4 1.5 bitcast_reduce_fusion.2
  359.2 1.5 convolution_add_fusion.2
  362.6 1.5 convolution_add_fusion.2
  365.9 1.5 convolution_add_fusion.2
  372.7 1.5 convolution_add_fusion.2
  376.0 1.5 convolution_add_fusion.2
  382.7 1.5 convolution_add_fusion.2
  386.1 1.5 convolution_add_fusion.2
  392.8 1.5 convolution_add_fusion.2
  396.2 1.5 convolution_add_fusion.2
  402.9 1.5 convolution_add_fusion.2
  406.3 1.5 convolution_add_fusion.2
  413.0 1.5 convolution_add_fusion.2
  416.3 1.5 convolution_add_fusion.2
  423.1 1.5 convolution_add_fusion.2
  426.4 1.5 convolution_add_fusion.2
  465.2 3.8 fusion.22
  469.0 4.4 copy.33
  475.8 355.9 %all-reduce = f32[256,16]{1,0:T(8,128)S(1)} all-reduce(f32[256,16]{1,0:T(8,128)S(1)} %fusion.37), channel_id=4, replica_groups=mesh['seq'=64,'head'=4] {'seq'}, use_global_device_ids=true, to_apply=%region_6.7.clone | all-reduce | flops 4096 | bytes 32768
  831.7 9.3 reduce-scatter.2.cloned.1.call-done
  842.9 34.6 %all-reduce.3.cloned.1.call-done = bf16[64,1024]{1,0:T(8,128)(2,1)} async-done(((bf16[64,1024]{1,0:T(8,128)(2,1)}), bf16[64,1024]{1,0:T(8,128)(2,1)}) %all-reduce.3.cloned.1.call-update) | async-done | bytes 131088 | tf_op jit(solution)/shard_map/psum | solution.py:90
  880.8 119.5 %all-gather.10.cloned.1.call-done = bf16[256,16,256]{2,1,0:T(8,128)(2,1)} async-done(((bf16[4,16,256]{2,1,0:T(8,128)(2,1)}), bf16[256,16,256]{2,1,0:T(8,128)(2,1)}) %all-gather.10.cloned.1.call-update) | async-done | bytes 2097168 | tf_op jit(solution)/shard_map/all_gather | solution.py:101
  1000.4 2.3 fusion.17
  1003.5 568.6 %all-gather.12.cloned.1.call-done = f32[16384,1024]{1,0:T(8,128)} async-done(((f32[256,1024]{1,0:T(8,128)}), f32[16384,1024]{1,0:T(8,128)}) %all-gather.12.cloned.1.call-update) | async-done | bytes 67108880 | tf_op jit(solution)/shard_map/all_gather | solution.py:110
  1572.1 21.6 %reduce_sum.28 = bf16[256,1024]{1,0:T(8,128)(2,1)} reduce(f32[64,256,1024]{2,1,0:T(8,128)} %bitcast.7, f32[]{:T(128)} %constant.12.clone.1), dimensions={0}, to_apply=%region_8.9 | reduce | flops 16515072 | bytes 67633152 | tf_op jit(solution)/shard_map/reduce_sum | solution.py:110
  (219 shorter events, 94.6 us)
Async XLA Ops:
  7.2 834.7 %copy-start = (bf16[256,1024]{1,0:T(8,128)(2,1)S(1)}, bf16[256,1024]{1,0:T(8,128)(2,1)}, u32[]{:S(2)}) copy-start(bf16[256,1024]{1,0:T(8,128)(2,1)} %param.15) | copy-start | bytes 1572868
  7.2 153.7 %all-gather.8.cloned.1.call-start = ((), (), s32[]{:S(2)}) async-start(), calls=%async_computation.2 | async-start | bytes 8519680 | tf_op jit(solution)/shard_map/all_gather | solution.py:48
  7.9 300.7 %all-gather.6.cloned.1.call-start = ((), (), s32[]{:S(2)}) async-start(), calls=%async_computation.1 | async-start | bytes 8519680 | tf_op jit(solution)/shard_map/all_gather | solution.py:47
  8.7 832.3 %reduce-scatter.2.cloned.1.call-start = ((), (), s32[]{:S(2)}) async-start(), calls=%async_computation.3 | async-start | bytes 4259840 | tf_op jit(solution)/shard_map/reduce_scatter | solution.py:84
  357.3 107.7 %copy-start.2 = (bf16[256,256]{1,0:T(8,128)(2,1)S(1)}, bf16[256,256]{1,0:T(8,128)(2,1)}, u32[]{:S(2)}) copy-start(bf16[256,256]{1,0:T(8,128)(2,1)} %param.14) | copy-start | bytes 393220
  357.3 107.8 %copy-start.3 = (s32[2,128]{1,0:T(2,128)S(1)}, s32[2,128]{1,0:T(2,128)}, u32[]{:S(2)}) copy-start(s32[2,128]{1,0:T(2,128)} %param.19) | copy-start | bytes 3076
  473.4 0.7 copy-start.4
  473.4 404.1 %copy-start.1 = (bf16[4,16,1024]{2,1,0:T(8,128)(2,1)S(1)}, bf16[4,16,1024]{2,1,0:T(8,128)(2,1)}, u32[]{:S(2)}) copy-start(bf16[4,16,1024]{2,1,0:T(8,128)(2,1)} %param.16) | copy-start | bytes 393220
  473.4 404.1 %all-reduce.3.cloned.1.call-start = ((), (), s32[]{:S(2)}) async-start(), calls=%async_computation.4 | async-start | bytes 262144 | tf_op jit(solution)/shard_map/psum | solution.py:90
  842.8 157.6 %all-gather.10.cloned.1.call-start = ((), (), s32[]{:S(2)}) async-start(), calls=%async_computation.5 | async-start | bytes 2129920 | tf_op jit(solution)/shard_map/all_gather | solution.py:101
  879.5 692.6 %all-gather.12.cloned.1.call-start = ((), (), s32[]{:S(2)}) async-start(), calls=%async_computation.6 | async-start | bytes 68157440 | tf_op jit(solution)/shard_map/all_gather | solution.py:110
Sparse Core Ops, SparseCore 0:
  11.7 149.1 all-gather.7
  164.5 144.0 all-gather.5
  473.5 367.3 reduce-scatter.1
  844.2 33.2 all-reduce.2
  881.6 118.6 all-gather.9
  1003.9 568.1 all-gather.11
